TPU v7x, 256 devices: a whole 4x4x8 slice. The times are simulated.
256 devices in a mesh: dp: 8 (over z), cls: 32 (over y, x, core).
Axes of the slice: x: 4, y: 4, z: 8, core: 2. Of those that a mesh axis runs over, the one named last changes fastest.
Arguments:
- weak_embed: bfloat16 [512, 512], P('dp'), may hold values from -6 to 6
- strong_embed: bfloat16 [512, 512], P('dp'), may hold values from -0.0625 to 0.0625
- centers: bfloat16 [1048576, 512], P(('dp', 'cls')), may hold values from -0.0625 to 0.0625
- marginal: float32 [1048576], P(('dp', 'cls')), may hold values from 0.25 to 45
- pseudo_label: int32 [512], P('dp'), may hold values from 0 to 1048575
- confident: int32 [512], P('dp'), may hold values 0 or 1
Outputs:
- new_marginal: float32 [1048576], P(('dp', 'cls'))
- center_grad: bfloat16 [1048576, 512], P(('dp', 'cls'))
- embed_grad: float32 [512, 512], P('dp')
- loss: float32 [], replicated
All inputs are finite; a program needn't handle non-finite values. No bound on the sum of `confident` on one device may be relied on, other than what follows from the above.
Results may differ from a plain program's by a relative error of at most 0.00155.
The roundings to bfloat16 on the way count: a program that leaves them out, or rounds other values in their place, can miss the bound.
Values may be sent and summed in bfloat16 or wider, within the bound.
A program may use at most 128 MiB of HBM per device.

v0:
```python
import jax
import jax.numpy as jnp
from jax import lax
from jax.sharding import PartitionSpec as P

SCALE = 64.0
MARGIN = 0.35
MOMENTUM = 0.9
EPS = 1e-06


def unit_rows(values):
    exact = values.astype(jnp.float32)
    inverse = lax.rsqrt(jnp.sum(exact * exact, axis=-1, keepdims=True) + EPS)
    return (exact * inverse, inverse)


def body(weak_embed, strong_embed, centers, marginal, pseudo_label, confident):
    img = strong_embed.shape[0]
    cls_dev = centers.shape[0]
    weak_exact, _ = unit_rows(weak_embed)
    strong_exact, strong_inv = unit_rows(strong_embed)
    stacked = jnp.stack([weak_exact.astype(jnp.bfloat16), strong_exact.astype(jnp.bfloat16)])
    views, labels, flag_ints = (
        lax.all_gather(stacked, "dp", axis=1, tiled=True),
        lax.all_gather(pseudo_label, "dp", axis=0, tiled=True),
        lax.all_gather(confident, "dp", axis=0, tiled=True),
    )
    row_count = views.shape[1]
    width = views.shape[2]
    flags = flag_ints.astype(jnp.float32)
    center_exact, center_inv = unit_rows(centers)
    center_unit = center_exact.astype(jnp.bfloat16)
    scores = lax.dot_general(
        views.reshape(2 * row_count, width),
        center_unit,
        (((1,), (1,)), ((), ())),
        preferred_element_type=jnp.float32,
    )
    teach = jnp.exp(SCALE * (scores[:row_count] - 1.0))
    offset = (lax.axis_index("dp") * lax.axis_size("cls") + lax.axis_index("cls")) * cls_dev
    ids = offset + jnp.arange(cls_dev, dtype=jnp.int32)
    hit = (labels[:, None] == ids[None, :]).astype(jnp.float32)
    stud = SCALE * (scores[row_count:] - MARGIN * hit)
    teach_part = jnp.sum(teach, axis=1)
    stud_part = jnp.sum(jnp.exp(stud - SCALE), axis=1)
    label_part = jnp.sum(hit * stud, axis=1)
    classes_total = cls_dev * lax.axis_size("dp") * lax.axis_size("cls")
    teacher_total = lax.psum(teach_part, ("dp", "cls"))
    share = teach / teacher_total[:, None]
    batch = classes_total / row_count * jnp.sum(share, axis=0)
    fresh = MOMENTUM * marginal + (1.0 - MOMENTUM) * batch
    raw = share / fresh[None, :]
    fresh, raw, q_part, r_part = (fresh, raw, jnp.sum(raw, axis=1), jnp.sum(raw * stud, axis=1))
    aligned_total, aligned_cross = lax.psum((q_part, r_part), ("dp", "cls"))
    student_total, label_logit = lax.psum((stud_part, label_part), ("dp", "cls"))
    loss = (
        jnp.sum(
            flags
            * (
                SCALE
                + jnp.log(student_total)
                - 0.5 * label_logit
                - 0.5 * aligned_cross / aligned_total
            )
        )
        / img
    )
    grad = (
        SCALE
        / img
        * flags[:, None]
        * (
            jnp.exp(stud - SCALE) / student_total[:, None]
            - 0.5 * hit
            - 0.5 * raw / aligned_total[:, None]
        )
    )
    grad = grad.astype(jnp.bfloat16)
    unit_part = jnp.dot(grad, center_unit, preferred_element_type=jnp.float32)
    unit_total = lax.psum(unit_part, ("dp", "cls"))
    unit_grad = lax.dynamic_slice_in_dim(unit_total, lax.axis_index("dp") * img, img, 0)
    embed_grad = (
        unit_grad - strong_exact * jnp.sum(strong_exact * unit_grad, axis=1, keepdims=True)
    ) * strong_inv
    cgrad = lax.dot_general(
        grad, views[1], (((0,), (0,)), ((), ())), preferred_element_type=jnp.float32
    )
    cgrad = (
        cgrad - center_exact * jnp.sum(center_exact * cgrad, axis=1, keepdims=True)
    ) * center_inv
    return (fresh, cgrad.astype(jnp.bfloat16), embed_grad, loss)


def solution(mesh):
    placed = (
        P("dp", None),
        P("dp", None),
        P(("dp", "cls"), None),
        P(("dp", "cls")),
        P("dp"),
        P("dp"),
    )
    return jax.shard_map(
        body,
        mesh=mesh,
        in_specs=placed,
        out_specs=(P(("dp", "cls")), P(("dp", "cls"), None), P("dp", None), P()),
        check_vma=False,
    )
```

profile of v0, /device:TPU:2, one launch (start us, length us, event | category | flops | bytes accessed | tf_op | source)
XLA Modules:
  0.0 508.1 jit_solution(5591353796502979499)
XLA Ops:
  7.2 0.0 copy-start.10
  7.2 0.0 copy-start.8
  7.2 0.0 copy-start.9
  7.2 0.0 all-gather.2.cloned.1.call-start
  7.2 1.0 fusion.32
  8.2 1.0 fusion.27
  9.2 1.0 fusion.33
  10.2 0.7 pad_maximum_fusion
  10.8 0.0 all-gather.2.cloned.1.call-update
  10.9 0.0 all-reduce.6.cloned.1.call-start
  10.9 6.3 %copy.10 = bf16[4096,512]{0,1:T(8,128)(2,1)} copy(bf16[4096,512]{1,0:T(8,128)(2,1)} %param.8) | data formatting | bytes 8388608 | tf_op args[2]
  17.2 0.0 copy-done.10
  17.2 0.6 dynamic-slice
  18.5 0.0 copy-done.8
  18.5 0.2 dynamic-update-slice
  18.7 0.0 copy-done.9
  18.7 0.2 dynamic-update-slice.1
  19.0 16.2 %all-reduce.2 = (s32[512]{0:T(512)S(1)}, s32[512]{0:T(512)S(1)}) all-reduce(s32[512]{0:T(512)S(1)} %dynamic-update-slice.1, s32[512]{0:T(512)S(1)} %dynamic-update-slice), channel_id=1, replica_groups=mesh['dp'=8,'cls'=32] {'dp'}, use_global_device_ids=true, to_apply=%add.1 | all-reduce | flops 1024 | bytes 8192
  35.2 3.1 fusion.7
  38.3 14.4 %all-gather.2.cloned.1.call-done = bf16[2,512,512]{2,1,0:T(8,128)(2,1)} async-done(((bf16[2,64,512]{2,1,0:T(8,128)(2,1)}), bf16[2,512,512]{2,1,0:T(8,128)(2,1)}) %all-gather.2.cloned.1.call-update) | async-done | bytes 1048592 | tf_op jit(solution)/shard_map/all_gather | solution.py:25
  52.7 6.6 %fusion.21 = f32[1024,4096]{1,0:T(8,128)S(1)} fusion(bf16[1024,512]{1,0:T(8,128)(2,1)} %bitcast.14, bf16[4096,512]{0,1:T(8,128)(2,1)} %copy.10, f32[4096]{0:T(1024)S(1)} %add_rsqrt_fusion), kind=kOutput, calls=%fused_computation.30 | convolution fusion | flops 4301258752 | bytes 22036480 | tf_op jit(solution)/shard_map/dot_general | solution.py:34
  59.3 0.0 copy-start
  59.3 5.7 %copy-done = f32[1024,4096]{1,0:T(8,128)} copy-done((f32[1024,4096]{1,0:T(8,128)}, f32[1024,4096]{1,0:T(8,128)S(1)}, u32[]{:S(2)}) %copy-start) | copy-done | bytes 16777240
  65.0 1.5 fusion.18
  66.5 74.2 %psum.42 = f32[512]{0:T(512)S(1)} all-reduce(f32[512]{0:T(512)S(1)} %fusion.18), channel_id=1, replica_groups=mesh['dp'=8,'cls'=32] {'dp','cls'}, use_global_device_ids=true, to_apply=%region_4.0 | all-reduce | flops 512 | bytes 4096 | tf_op jit(solution)/shard_map/psum | solution.py:49
  140.8 4.4 divide_reduce_fusion
  145.1 0.0 copy-done.6
  145.2 0.0 copy-start.5
  145.2 10.2 %fusion.14 = (f32[512]{0:T(512)S(1)}, f32[512]{0:T(512)S(1)}, f32[512]{0:T(512)S(1)}, f32[512]{0:T(512)S(1)}) fusion(s32[4096]{0:T(1024)S(1)} %iota_add_fusion, s32[512]{0:T(512)S(1)} %get-tuple-element.12, f32[1024,4096]{1,0:T(8,128)} %copy-done, f32[4096]{0:T(1024)S(1)} %multiply_add_fusion, f32[512]{0:T(512)S(1)} %psum.42), kind=kLoop, calls=%fused_computation.19 | loop fusion | flops 31455232 | bytes 16822272 | tf_op jit(solution)/shard_map/reduce_sum | solution.py:47
  155.4 73.8 %all-reduce.3 = (f32[512]{0:T(512)S(1)}, f32[512]{0:T(512)S(1)}, f32[512]{0:T(512)S(1)}, f32[512]{0:T(512)S(1)}) all-reduce(f32[512]{0:T(512)S(1)} %get-tuple-element.10, f32[512]{0:T(512)S(1)} %get-tuple-element.11, f32[512]{0:T(512)S(1)} %get-tuple-element.9, f32[512]{0:T(512)S(1)} %get-tuple-element.8), channel_id=1, replica_groups=mesh['dp'=8,'cls'=32] {'dp','cls'}, use_global_device_ids=true, to_apply=%region_9.0 | all-reduce | flops 2048 | bytes 16384 | tf_op jit(solution)/shard_map/psum | solution.py:55
  229.2 0.0 copy-done.5
  229.2 9.6 %fusion.13 = bf16[512,4096]{1,0:T(8,128)(2,1)S(1)} fusion(f32[512]{0:T(512)S(1)} %get-tuple-element.14, f32[512]{0:T(512)S(1)} %get-tuple-element.15, s32[4096]{0:T(1024)S(1)} %iota_add_fusion, f32[512]{0:T(512)S(1)} %convert_element_type.34, s32[512]{0:T(512)S(1)} %get-tuple-element.12, f32[1024,4096]{1,0:T(8,128)} %copy-done, ...), kind=kLoop, calls=%fused_computation.18 | loop fusion | flops 35651584 | bytes 21014528 | tf_op jit(solution)/shard_map/convert_element_type | solution.py:79
  238.9 0.0 copy-start.3
  238.9 1.9 copy-done.3
  240.8 0.0 copy-done.1
  240.8 3.4 fusion.19
  244.2 0.0 all-reduce.6.cloned.1.call-update
  244.2 0.0 copy-done.7
  244.2 0.0 copy-start.2
  244.2 6.4 %fusion.3 = (f32[4096]{0:T(1024)S(1)}, f32[4096,512]{0,1:T(8,128)S(1)}) fusion(bf16[4096,512]{0,1:T(8,128)(2,1)} %copy.10, f32[4096]{0:T(1024)S(1)} %add_rsqrt_fusion, bf16[512,4096]{1,0:T(8,128)(2,1)} %copy-done.3, bf16[2,512,512]{2,1,0:T(8,128)(2,1)S(1)} %copy-done.7), kind=kOutput, calls=%fused_computation.8 | convolution fusion | flops 2155868160 | bytes 17334272 | tf_op jit(solution)/shard_map/dot_general | solution.py:86
  250.7 0.0 copy-done.2
  250.7 3.5 fusion.6
  254.2 6.4 %copy.11 = bf16[4096,512]{1,0:T(8,128)(2,1)} copy(bf16[4096,512]{0,1:T(8,128)(2,1)} %fusion.6) | data formatting | bytes 8388608
  260.6 0.6 multiply_reduce_fusion.1
  261.9 235.5 %all-reduce.6.cloned.1.call-done = f32[512,512]{1,0:T(8,128)} async-done(((f32[512,512]{1,0:T(8,128)}), f32[512,512]{1,0:T(8,128)}) %all-reduce.6.cloned.1.call-update) | async-done | bytes 1048592 | tf_op jit(solution)/shard_map/psum | solution.py:81
  497.4 0.0 copy-done.4
  497.4 1.1 fusion.29
  498.5 1.7 fusion.31
  (12 shorter events, 0.0 us)
Async XLA Ops:
  7.2 10.1 %copy-start.10 = (u32[256]{0:T(256)S(1)}, u32[256]{0:T(256)}, u32[]{:S(2)}) copy-start(u32[256]{0:T(256)} %constant.51) | copy-start | bytes 3076
  7.2 11.3 %copy-start.8 = (s32[64]{0:T(128)S(1)}, s32[64]{0:T(128)}, u32[]{:S(2)}) copy-start(s32[64]{0:T(128)} %param.11) | copy-start | bytes 772
  7.2 11.6 %copy-start.9 = (s32[64]{0:T(128)S(1)}, s32[64]{0:T(128)}, u32[]{:S(2)}) copy-start(s32[64]{0:T(128)} %param.10) | copy-start | bytes 772
  7.2 45.5 %all-gather.2.cloned.1.call-start = ((), (), s32[]{:S(2)}) async-start(), calls=%async_computation | async-start | bytes 1179648 | tf_op jit(solution)/shard_map/all_gather | solution.py:25
  10.9 486.5 %all-reduce.6.cloned.1.call-start = ((), (), s32[]{:S(2)}) async-start(), calls=%async_computation.1 | async-start | bytes 2097152 | tf_op jit(solution)/shard_map/psum | solution.py:81
  59.3 5.7 %copy-start = (f32[1024,4096]{1,0:T(8,128)}, f32[1024,4096]{1,0:T(8,128)S(1)}, u32[]{:S(2)}) copy-start(f32[1024,4096]{1,0:T(8,128)S(1)} %fusion.21) | copy-start | bytes 50331652
  65.0 80.1 %copy-start.6 = (f32[4096]{0:T(1024)S(1)}, f32[4096]{0:T(1024)}, u32[]{:S(2)}) copy-start(f32[4096]{0:T(1024)} %param.9) | copy-start | bytes 49156
  145.2 84.0 %copy-start.5 = (f32[4096]{0:T(1024)}, f32[4096]{0:T(1024)S(1)}, u32[]{:S(2)}) copy-start(f32[4096]{0:T(1024)S(1)} %multiply_add_fusion) | copy-start | bytes 49156
  229.2 11.6 %copy-start.1 = (bf16[4096,512]{0,1:T(8,128)(2,1)S(1)}, bf16[4096,512]{0,1:T(8,128)(2,1)}, u32[]{:S(2)}) copy-start(bf16[4096,512]{0,1:T(8,128)(2,1)} %copy.10) | copy-start | bytes 12582916
  238.9 1.9 copy-start.3
  240.8 3.4 copy-start.7
  244.2 6.5 %copy-start.2 = (bf16[4096,512]{0,1:T(8,128)(2,1)S(1)}, bf16[4096,512]{0,1:T(8,128)(2,1)}, u32[]{:S(2)}) copy-start(bf16[4096,512]{0,1:T(8,128)(2,1)} %copy.10) | copy-start | bytes 12582916
  254.2 243.2 %copy-start.4 = (bf16[64,512]{1,0:T(8,128)(2,1)S(1)}, bf16[64,512]{1,0:T(8,128)(2,1)}, u32[]{:S(2)}) copy-start(bf16[64,512]{1,0:T(8,128)(2,1)} %param.7) | copy-start | bytes 196612
Sparse Core Ops, SparseCore 0:
  11.0 41.6 all-gather.1
  244.3 252.9 all-reduce.5
where the time goes:
time: 509 us; the launch traced here: 508 us
  waiting for transfers between devices  250 us (49%)
  blocking collectives  164 us (32%)
  other arithmetic  39.3 us (8%)
  local copies, waits for them, and re-layouts  21.5 us (4%)
  between operations  16.7 us (3%)
  matrix products  16.4 us (3%)
    psum x1, waiting for transfers between devices, body(): unit_total = lax.psum(unit_part, ('dp', 'cls'))  235 us
    psum x1, blocking collectives, body(): teacher_total = lax.psum(teach_part, ('dp', 'cls'))  74.2 us
    psum x1, blocking collectives, body(): aligned_total, aligned_cross = lax.psum((q_part, r_part), ('dp', 'cls'))  73.8 us
    unnamed x29, local copies, waits for them, and re-layouts  21.5 us
    unnamed x1, blocking collectives  16.2 us
    all_gather x1, waiting for transfers between devices, body(): lax.all_gather(stacked, 'dp', axis=1, tiled=True)  14.4 us
    reduce_sum x1, other arithmetic, body(): label_part = jnp.sum(hit * stud, axis=1)  10.2 us
  transfers between devices with their start and end apart: 2, of which 2 were waited for; matrix products, arithmetic and copies ran while one was open for 5% of the time, Pallas kernels for 0%

commit v1 on v0

--- a/solution.py
+++ b/solution.py
@@ -46,7 +46,7 @@
     stud_part = jnp.sum(jnp.exp(stud - SCALE), axis=1)
     label_part = jnp.sum(hit * stud, axis=1)
     classes_total = cls_dev * lax.axis_size("dp") * lax.axis_size("cls")
-    teacher_total = lax.psum(teach_part, ("dp", "cls"))
+    teacher_total = jnp.sum(lax.all_gather(teach_part, ("dp", "cls")), axis=0)
     share = teach / teacher_total[:, None]
     batch = classes_total / row_count * jnp.sum(share, axis=0)
     fresh = MOMENTUM * marginal + (1.0 - MOMENTUM) * batch

time: 509 us -> 503 us (0.988)
  blocking collectives: 164 us -> 158 us
    psum x1 -> x0, blocking collectives: 74.2 us -> none  [body(): teacher_total = lax.psum(teach_part, ('dp', 'cls'))]
    all_gather x0 -> x1, blocking collectives: none -> 66.6 us  [body(): teacher_total = jnp.sum(lax.all_gather(teach_part, ('dp', 'cls')), axis=0)]
where the time goes in v1:
time: 503 us; the launch traced here: 502 us
  waiting for transfers between devices  250 us (50%)
  blocking collectives  158 us (31%)
  other arithmetic  39.6 us (8%)
  local copies, waits for them, and re-layouts  21.5 us (4%)
  between operations  16.7 us (3%)
  matrix products  16.4 us (3%)
    psum x1, waiting for transfers between devices, body(): unit_total = lax.psum(unit_part, ('dp', 'cls'))  236 us
    psum x1, blocking collectives, body(): aligned_total, aligned_cross = lax.psum((q_part, r_part), ('dp', 'cls'))  74.8 us
    all_gather x1, blocking collectives, body(): teacher_total = jnp.sum(lax.all_gather(teach_part, ('dp', 'cls')), axis=0)  66.6 us
    unnamed x29, local copies, waits for them, and re-layouts  21.5 us
    unnamed x1, blocking collectives  16.2 us
    all_gather x1, waiting for transfers between devices, body(): lax.all_gather(stacked, 'dp', axis=1, tiled=True)  14.4 us
    reduce_sum x1, other arithmetic, body(): label_part = jnp.sum(hit * stud, axis=1)  10.2 us
  transfers between devices with their start and end apart: 2, of which 2 were waited for; matrix products, arithmetic and copies ran while one was open for 5% of the time, Pallas kernels for 0%

profile of v1, /device:TPU:2, one launch (start us, length us, event | category | flops | bytes accessed | tf_op | source)
XLA Modules:
  0.0 502.0 jit_solution(6218699096904499758)
XLA Ops:
  7.2 0.0 copy-start.10
  7.2 0.0 copy-start.8
  7.2 0.0 copy-start.9
  7.2 0.0 all-gather.4.cloned.1.call-start
  7.2 1.0 fusion.32
  8.2 1.0 fusion.27
  9.2 1.0 fusion.33
  10.2 0.7 pad_maximum_fusion
  10.8 0.0 all-gather.4.cloned.1.call-update
  10.9 0.0 all-reduce.6.cloned.1.call-start
  10.9 6.3 %copy.12 = bf16[4096,512]{0,1:T(8,128)(2,1)} copy(bf16[4096,512]{1,0:T(8,128)(2,1)} %param.8) | data formatting | bytes 8388608 | tf_op args[2]
  17.2 0.0 copy-done.10
  17.2 0.6 dynamic-slice
  18.5 0.0 copy-done.8
  18.5 0.2 dynamic-update-slice
  18.7 0.0 copy-done.9
  18.7 0.2 dynamic-update-slice.1
  19.0 16.2 %all-reduce.2 = (s32[512]{0:T(512)S(1)}, s32[512]{0:T(512)S(1)}) all-reduce(s32[512]{0:T(512)S(1)} %dynamic-update-slice.1, s32[512]{0:T(512)S(1)} %dynamic-update-slice), channel_id=1, replica_groups=mesh['dp'=8,'cls'=32] {'dp'}, use_global_device_ids=true, to_apply=%add.1 | all-reduce | flops 1024 | bytes 8192
  35.2 3.1 fusion.7
  38.3 14.4 %all-gather.4.cloned.1.call-done = bf16[2,512,512]{2,1,0:T(8,128)(2,1)} async-done(((bf16[2,64,512]{2,1,0:T(8,128)(2,1)}), bf16[2,512,512]{2,1,0:T(8,128)(2,1)}) %all-gather.4.cloned.1.call-update) | async-done | bytes 1048592 | tf_op jit(solution)/shard_map/all_gather | solution.py:25
  52.7 6.6 %fusion.21 = f32[1024,4096]{1,0:T(8,128)S(1)} fusion(bf16[1024,512]{1,0:T(8,128)(2,1)} %bitcast.16, bf16[4096,512]{0,1:T(8,128)(2,1)} %copy.12, f32[4096]{0:T(1024)S(1)} %add_rsqrt_fusion), kind=kOutput, calls=%fused_computation.30 | convolution fusion | flops 4301258752 | bytes 22036480 | tf_op jit(solution)/shard_map/dot_general | solution.py:34
  59.3 0.0 copy-start
  59.3 5.7 %copy-done = f32[1024,4096]{1,0:T(8,128)} copy-done((f32[1024,4096]{1,0:T(8,128)}, f32[1024,4096]{1,0:T(8,128)S(1)}, u32[]{:S(2)}) %copy-start) | copy-done | bytes 16777240
  65.0 1.5 fusion.18
  66.5 66.6 %all-gather.1 = f32[256,1,512]{2,1,0:T(1,128)S(1)} all-gather(f32[1,1,512]{2,1,0:T(1,128)S(1)} %bitcast.15), channel_id=2, replica_groups=mesh['dp'=8,'cls'=32] {'dp','cls'}, dimensions={0}, use_global_device_ids=true | all-gather | bytes 526336 | tf_op jit(solution)/shard_map/all_gather | solution.py:49
  133.2 0.3 reduce_sum.121
  133.5 4.4 divide_reduce_fusion
  137.9 0.0 copy-done.6
  137.9 0.0 copy-start.5
  138.0 10.2 %fusion.14 = (f32[512]{0:T(512)S(1)}, f32[512]{0:T(512)S(1)}, f32[512]{0:T(512)S(1)}, f32[512]{0:T(512)S(1)}) fusion(s32[4096]{0:T(1024)S(1)} %iota_add_fusion, s32[512]{0:T(512)S(1)} %get-tuple-element.16, f32[1024,4096]{1,0:T(8,128)} %copy-done, f32[4096]{0:T(1024)S(1)} %multiply_add_fusion, f32[512]{0:T(512)S(1)} %reduce_sum.121), kind=kLoop, calls=%fused_computation.19 | loop fusion | flops 31455232 | bytes 16822272 | tf_op jit(solution)/shard_map/reduce_sum | solution.py:47
  148.2 74.8 %all-reduce.3 = (f32[512]{0:T(512)S(1)}, f32[512]{0:T(512)S(1)}, f32[512]{0:T(512)S(1)}, f32[512]{0:T(512)S(1)}) all-reduce(f32[512]{0:T(512)S(1)} %get-tuple-element.14, f32[512]{0:T(512)S(1)} %get-tuple-element.15, f32[512]{0:T(512)S(1)} %get-tuple-element.13, ...), channel_id=1, replica_groups=mesh['dp'=8,'cls'=32] {'dp','cls'}, use_global_device_ids=true, to_apply=%region_9.0 | all-reduce | flops 2048 | bytes 16384 | tf_op jit(solution)/shard_map/psum | solution.py:55
  223.0 0.0 copy-done.5
  223.0 9.6 %fusion.13 = bf16[512,4096]{1,0:T(8,128)(2,1)S(1)} fusion(f32[512]{0:T(512)S(1)} %get-tuple-element.18, f32[512]{0:T(512)S(1)} %get-tuple-element.19, s32[4096]{0:T(1024)S(1)} %iota_add_fusion, f32[512]{0:T(512)S(1)} %convert_element_type.34, s32[512]{0:T(512)S(1)} %get-tuple-element.16, f32[1024,4096]{1,0:T(8,128)} %copy-done, ...), kind=kLoop, calls=%fused_computation.18 | loop fusion | flops 35651584 | bytes 21014528 | tf_op jit(solution)/shard_map/convert_element_type | solution.py:79
  232.6 0.0 copy-start.3
  232.6 1.9 copy-done.3
  234.6 0.0 copy-done.1
  234.6 3.4 fusion.19
  238.0 0.0 all-reduce.6.cloned.1.call-update
  238.0 0.0 copy-done.7
  238.0 0.0 copy-start.2
  238.0 6.4 %fusion.3 = (f32[4096]{0:T(1024)S(1)}, f32[4096,512]{0,1:T(8,128)S(1)}) fusion(bf16[4096,512]{0,1:T(8,128)(2,1)} %copy.12, f32[4096]{0:T(1024)S(1)} %add_rsqrt_fusion, bf16[512,4096]{1,0:T(8,128)(2,1)} %copy-done.3, bf16[2,512,512]{2,1,0:T(8,128)(2,1)S(1)} %copy-done.7), kind=kOutput, calls=%fused_computation.8 | convolution fusion | flops 2155868160 | bytes 17334272 | tf_op jit(solution)/shard_map/dot_general | solution.py:86
  244.4 0.0 copy-done.2
  244.5 3.5 fusion.6
  248.0 6.4 %copy.13 = bf16[4096,512]{1,0:T(8,128)(2,1)} copy(bf16[4096,512]{0,1:T(8,128)(2,1)} %fusion.6) | data formatting | bytes 8388608
  254.4 0.6 multiply_reduce_fusion.1
  255.7 235.6 %all-reduce.6.cloned.1.call-done = f32[512,512]{1,0:T(8,128)} async-done(((f32[512,512]{1,0:T(8,128)}), f32[512,512]{1,0:T(8,128)}) %all-reduce.6.cloned.1.call-update) | async-done | bytes 1048592 | tf_op jit(solution)/shard_map/psum | solution.py:81
  491.3 1.1 fusion.29
  492.4 1.7 fusion.31
  (13 shorter events, 0.0 us)
Async XLA Ops:
  7.2 10.1 %copy-start.10 = (u32[256]{0:T(256)S(1)}, u32[256]{0:T(256)}, u32[]{:S(2)}) copy-start(u32[256]{0:T(256)} %constant.51) | copy-start | bytes 3076
  7.2 11.3 %copy-start.8 = (s32[64]{0:T(128)S(1)}, s32[64]{0:T(128)}, u32[]{:S(2)}) copy-start(s32[64]{0:T(128)} %param.11) | copy-start | bytes 772
  7.2 11.6 %copy-start.9 = (s32[64]{0:T(128)S(1)}, s32[64]{0:T(128)}, u32[]{:S(2)}) copy-start(s32[64]{0:T(128)} %param.10) | copy-start | bytes 772
  7.2 45.5 %all-gather.4.cloned.1.call-start = ((), (), s32[]{:S(2)}) async-start(), calls=%async_computation | async-start | bytes 1179648 | tf_op jit(solution)/shard_map/all_gather | solution.py:25
  10.9 480.4 %all-reduce.6.cloned.1.call-start = ((), (), s32[]{:S(2)}) async-start(), calls=%async_computation.1 | async-start | bytes 2097152 | tf_op jit(solution)/shard_map/psum | solution.py:81
  59.3 5.7 %copy-start = (f32[1024,4096]{1,0:T(8,128)}, f32[1024,4096]{1,0:T(8,128)S(1)}, u32[]{:S(2)}) copy-start(f32[1024,4096]{1,0:T(8,128)S(1)} %fusion.21) | copy-start | bytes 50331652
  65.0 72.9 %copy-start.6 = (f32[4096]{0:T(1024)S(1)}, f32[4096]{0:T(1024)}, u32[]{:S(2)}) copy-start(f32[4096]{0:T(1024)} %param.9) | copy-start | bytes 49156
  137.9 85.1 %copy-start.5 = (f32[4096]{0:T(1024)}, f32[4096]{0:T(1024)S(1)}, u32[]{:S(2)}) copy-start(f32[4096]{0:T(1024)S(1)} %multiply_add_fusion) | copy-start | bytes 49156
  223.0 11.6 %copy-start.1 = (bf16[4096,512]{0,1:T(8,128)(2,1)S(1)}, bf16[4096,512]{0,1:T(8,128)(2,1)}, u32[]{:S(2)}) copy-start(bf16[4096,512]{0,1:T(8,128)(2,1)} %copy.12) | copy-start | bytes 12582916
  232.6 1.9 copy-start.3
  234.6 3.4 copy-start.7
  238.0 6.5 %copy-start.2 = (bf16[4096,512]{0,1:T(8,128)(2,1)S(1)}, bf16[4096,512]{0,1:T(8,128)(2,1)}, u32[]{:S(2)}) copy-start(bf16[4096,512]{0,1:T(8,128)(2,1)} %copy.12) | copy-start | bytes 12582916
  248.0 243.3 %copy-start.4 = (bf16[64,512]{1,0:T(8,128)(2,1)S(1)}, bf16[64,512]{1,0:T(8,128)(2,1)}, u32[]{:S(2)}) copy-start(bf16[64,512]{1,0:T(8,128)(2,1)} %param.7) | copy-start | bytes 196612
Sparse Core Ops, SparseCore 0:
  11.0 41.6 all-gather.3
  238.1 253.1 all-reduce.5
